TPU v7x, 128 devices: a whole 4x4x4 slice. The times are simulated.
128 devices in a mesh: clus: 128 (over y, z, x, core).
Axes of the slice: x: 4, y: 4, z: 4, core: 2. Of those that a mesh axis runs over, the one named last changes fastest.
Arguments:
- charges: float32 [32, 1048576], P(None, 'clus'), may hold values from -6 to 6
- positions: float32 [3, 1048576], P(None, 'clus'), may hold values from -2 to 2
- quad_weights: float32 [1048576], P('clus'), may hold values from 0.1 to 1
- leaf_basis: float32 [4096, 64, 256], P('clus'), may hold values from -0.375 to 0.375
- leaf_nodes: float32 [3, 262144], P(None, 'clus'), may hold values from -2 to 2
- leaf_transfer: float32 [64, 262144], P(None, 'clus'), may hold values from -0.75 to 0.75
- mid_nodes: float32 [3, 8192], P(None, 'clus'), may hold values from -2 to 2
- mid_transfer: float32 [64, 8192], P(None, 'clus'), may hold values from -0.75 to 0.75
- top_nodes: float32 [3, 1024], replicated, may hold values from -2 to 2
- near_list: int32 [4096, 27], P('clus'), may hold values from 0 to 4095, as said below
- near_count: int32 [4096], P('clus'), may hold values from 1 to 27, as said below
- far_list: int32 [4096, 16], P('clus'), may hold values from 0 to 4095, as said below
- mid_mask: int32 [128, 128], P('clus'), may hold values 0 or 1
- top_mask: int32 [16, 16], replicated, may hold values 0 or 1
Outputs:
- potential: float32 [32, 1048576], P(None, 'clus')
Inputs may be any that keep to these rules, and one draw needn't show every extreme that they name: `near_list`: every entry names a leaf of the device that owns the row's leaf or of the device just before or after it in a cycle over devices (the last device's next one being the first); the entries of one row are distinct and differ from those of the row's far_list. `far_list`: the same locality holds: sources lie on the owning device or its two cyclic neighbours; entries of one row are distinct. `near_count`: some leaf has all 27 slots live in every draw.
All inputs are finite; a program needn't handle non-finite values. No bound on the sum of `mid_mask` on one device may be relied on, other than what follows from the above.
Results may differ from a plain program's by a relative error of at most 0.0003.
Values sent between devices are 32-bit elements; how exact they have to be, the bound alone decides.
No kernel may reach another device: no remote copies, remote signals or barrier semaphores. Data moves between devices by JAX's collectives and lax.ppermute only.
A program may use at most 128 MiB of HBM per device.

v0:
```python
import functools
import math

import jax
import jax.numpy as jnp
from jax import lax
from jax.experimental import pallas as pl
from jax.experimental.pallas import tpu as pltpu
from jax.sharding import PartitionSpec as P

LEAF = 256
RANK = 64
NRHS = 32
LEAF_DEV = 32
NEAR_MAX = 27
FAR2 = 16
GROUP = 8

STEP = 4
LIST = 1024
FEAT = 64
WIDE = STEP * LEAF
PACK = STEP * (LEAF + RANK)
GROUPS = 4
UNROLL = 16

smoothing = 0.05
inv_four_pi = 1.0 / (4.0 * math.pi)
highest = lax.Precision.HIGHEST
bf16 = jnp.bfloat16
f32 = jnp.float32
NN = (((1,), (0,)), ((), ()))
NT = (((1,), (1,)), ((), ()))
LIMIT = pltpu.CompilerParams(vmem_limit_bytes=63 * 2**20)
SMEM = pl.BlockSpec(memory_space=pltpu.SMEM)


def product(left, right, dims, precision=None):
    return lax.dot_general(left, right, dims, precision=precision, preferred_element_type=f32)


def source_rows(out, points):
    width = points.shape[1]
    out[0:3] = points
    out[3:4] = jnp.sum(points * points, axis=0, keepdims=True)
    out[4:5] = jnp.ones((1, width), f32)
    out[5:8] = jnp.zeros((3, width), f32)


def target_rows(out, points):
    width = points.shape[1]
    out[0:3] = points * -2.0
    out[3:4] = jnp.ones((1, width), f32)
    out[4:5] = jnp.sum(points * points, axis=0, keepdims=True) + smoothing * smoothing
    out[5:8] = jnp.zeros((3, width), f32)


def three(rows):
    first = rows.astype(bf16).astype(f32)
    rest = rows - first
    second = rest.astype(bf16).astype(f32)
    third = (rest - second).astype(bf16).astype(f32)
    return first, second, third


def source_features(rows):
    a, b, c = three(rows)
    return jnp.concatenate([a, a, b, a, c, b, b, c], axis=0)


def target_features(rows):
    a, b, c = three(rows)
    return jnp.concatenate([a, b, a, c, a, b, c, b], axis=0)


def two(values):
    high = values.astype(bf16)
    low = (values - high.astype(f32)).astype(bf16)
    return high, low


def fine(left, right, dims):
    rows = left.shape[0]
    high, low = two(left)
    near_high, near_low = two(right)
    both = product(jnp.concatenate([high, low], axis=0), near_high, dims)
    return both[0:rows] + both[rows : 2 * rows] + product(high, near_low, dims)


def whole(array):
    zeros = (0,) * array.ndim
    return pl.BlockSpec(array.shape, lambda i: zeros)


def upward_kernel(
    charges_ref,
    points_ref,
    weights_ref,
    basis_ref,
    nodes_ref,
    transfer_ref,
    mid_nodes_ref,
    mid_transfer_ref,
    pack_ref,
    target_ref,
    node_target_ref,
    level_ref,
    total,
    mid_rows,
):
    step = pl.program_id(0)

    @pl.when(step == 0)
    def _():
        total[...] = jnp.zeros_like(total)

    for group in range(GROUPS):
        wide = slice(group * WIDE, (group + 1) * WIDE)
        narrow = slice(group * STEP * RANK, (group + 1) * STEP * RANK)
        first = group * PACK
        charges = charges_ref[:, wide]
        pack_ref[0:NRHS, first : first + WIDE] = charges * (weights_ref[:, wide] * inv_four_pi)
        source_rows(pack_ref.at[NRHS : NRHS + 8, first : first + WIDE], points_ref[:, wide])
        target_rows(target_ref.at[:, wide], points_ref[:, wide])
        coefs = []
        for k in range(STEP):
            coefs.append(fine(charges[:, k * LEAF : (k + 1) * LEAF], basis_ref[group * STEP + k], NT))
        coef = jnp.concatenate(coefs, axis=1)
        pack_ref[0:NRHS, first + WIDE : first + PACK] = coef
        source_rows(pack_ref.at[NRHS : NRHS + 8, first + WIDE : first + PACK], nodes_ref[:, narrow])
        target_rows(node_target_ref.at[:, narrow], nodes_ref[:, narrow])
        total[...] += fine(coef, transfer_ref[:, narrow], NT)

    @pl.when(step == pl.num_programs(0) - 1)
    def _():
        mid_coef = total[...]
        top_coef = fine(mid_coef, mid_transfer_ref[...], NT)
        level_ref[0:NRHS] = jnp.concatenate([mid_coef, top_coef], axis=1)
        source_rows(mid_rows, mid_nodes_ref[...])
        level_ref[NRHS : NRHS + 8] = jnp.concatenate([mid_rows[...], jnp.zeros((8, RANK), f32)], axis=1)


def upward(charges, points, weights, basis, nodes, transfer, mid_nodes, mid_transfer):
    lanes = lambda rows, width: pl.BlockSpec((rows, width), lambda i: (0, i))
    fixed = lambda rows, width: pl.BlockSpec((rows, width), lambda i: (0, 0))
    wide, narrow, steps = GROUPS * WIDE, GROUPS * STEP * RANK, LEAF_DEV // (GROUPS * STEP)
    shape = jax.ShapeDtypeStruct
    return pl.pallas_call(
        upward_kernel,
        grid=(steps,),
        in_specs=[
            lanes(NRHS, wide),
            lanes(3, wide),
            lanes(1, wide),
            pl.BlockSpec((GROUPS * STEP, RANK, LEAF), lambda i: (i, 0, 0)),
            lanes(3, narrow),
            lanes(RANK, narrow),
            fixed(3, RANK),
            fixed(RANK, RANK),
        ],
        out_specs=[lanes(NRHS + 8, GROUPS * PACK), lanes(8, wide), lanes(8, narrow), fixed(NRHS + 8, 2 * RANK)],
        out_shape=[
            shape((NRHS + 8, steps * GROUPS * PACK), f32),
            shape((8, LEAF_DEV * LEAF), f32),
            shape((8, LEAF_DEV * RANK), f32),
            shape((NRHS + 8, 2 * RANK), f32),
        ],
        scratch_shapes=[pltpu.VMEM((NRHS, RANK), f32), pltpu.VMEM((8, RANK), f32)],
        compiler_params=LIMIT,
        name="upward",
    )(charges, points, weights, basis, nodes, transfer, mid_nodes, mid_transfer)


def lists_kernel(devices, near_ref, count_ref, far_list_ref, list_ref, far_ref):
    myself = lax.axis_index("clus")
    partner_step = jnp.where(myself % 2 == 0, 1, devices - 1)

    def place(leaves):
        steps = lax.shift_right_logical(leaves, 5) - myself
        steps = jnp.where(steps < 0, steps + devices, steps)
        return steps == 0, jnp.where(steps == partner_step, 0, LEAF_DEV) + (leaves & (LEAF_DEV - 1))

    own, other = place(far_list_ref[...])
    far_ref[...] = jnp.where(own, far_list_ref[...] & (LEAF_DEV - 1), other + LEAF_DEV)

    leaves = near_ref[...]
    own, other = place(leaves)
    row = lax.broadcasted_iota(jnp.int32, leaves.shape, 0)
    code = (lax.shift_left(row, 6) | jnp.where(own, leaves & (LEAF_DEV - 1), other)).astype(f32)
    square = (LEAF_DEV, LEAF_DEV)
    up, across = lax.broadcasted_iota(jnp.int32, square, 0), lax.broadcasted_iota(jnp.int32, square, 1)
    counts = jnp.sum(jnp.where(up == across, jnp.broadcast_to(count_ref[...], square), 0).astype(f32), axis=1, keepdims=True)
    live = lax.broadcasted_iota(jnp.int32, leaves.shape, 1).astype(f32) < counts
    slots = (NEAR_MAX, NEAR_MAX)
    earlier_slot = lax.broadcasted_iota(jnp.int32, slots, 0) < lax.broadcasted_iota(jnp.int32, slots, 1)
    earlier_slot = jnp.where(earlier_slot, 1.0, 0.0).astype(bf16)
    earlier_row = jnp.where(across < up, 1.0, 0.0).astype(bf16)
    mine = jnp.where(live, jnp.where(own, 1.0, 0.0), 0.0)
    marks = (mine, jnp.where(live, 1.0 - mine, 0.0))
    places, lengths = [], []
    for chosen in marks:
        mark = chosen.astype(bf16)
        before = jnp.sum(product(earlier_row, mark, NN), axis=1, keepdims=True)
        places.append(before + product(mark, earlier_slot, NN))
        lengths.append(jnp.sum(jnp.sum(chosen, axis=1, keepdims=True), axis=0, keepdims=True))
    spots = jnp.where(marks[0] > 0.0, places[0], jnp.where(marks[1] > 0.0, LIST - 1.0 - places[1], -1.0))
    for first in range(0, LIST, 256):
        spot = (lax.broadcasted_iota(jnp.int32, (1, 256), 1) + first).astype(f32)
        total = jnp.zeros((LEAF_DEV, 256), f32)
        for slot in range(NEAR_MAX):
            total = total + jnp.where(spots[:, slot : slot + 1] == spot, code[:, slot : slot + 1], 0.0)
        words = jnp.sum(total, axis=0, keepdims=True)
        filled = jnp.where(spot < lengths[0], 1.0, jnp.where(spot > LIST - 1.0 - lengths[1], 1.0, 0.0))
        words = jnp.where(filled > 0.0, words, float(LEAF_DEV << 6))
        list_ref[0:1, first : first + 256] = words.astype(jnp.int32)
    lane = lax.broadcasted_iota(jnp.int32, (1, LIST), 1)
    list_ref[1:2] = jnp.where(lane == 0, lengths[0], lengths[1]).astype(jnp.int32)


def lists(devices, near_list, near_count, far_list):
    operands = (near_list, near_count.reshape(1, -1), far_list)
    shapes = [jax.ShapeDtypeStruct((2, LIST), jnp.int32), jax.ShapeDtypeStruct(far_list.shape, jnp.int32)]
    return pl.pallas_call(
        functools.partial(lists_kernel, devices),
        grid=(1,),
        in_specs=[whole(operand) for operand in operands],
        out_specs=[whole(shape) for shape in shapes],
        out_shape=shapes,
        compiler_params=LIMIT,
        name="lists",
    )(*operands)


def far_field(far_ref, packs, node_target_ref, field_ref, highs, lows, nodes, coefs):
    lower = lax.broadcasted_iota(jnp.int32, (1, 2 * RANK), 1) < RANK

    for phase, ref in enumerate(packs):

        def prepare(group, _):
            for k in range(4):
                pair = group * 4 + k
                start = (group * 2 + k // 2) * PACK + WIDE + k % 2 * (2 * RANK)
                lanes = pl.ds(pl.multiple_of(start, 2 * RANK), 2 * RANK)
                features = source_features(ref[NRHS : NRHS + 8, lanes])
                turned = jnp.concatenate([features, features], axis=0).T
                coef = ref[0:NRHS, lanes]
                swapped = pltpu.roll(coef, RANK, 1)
                for half in range(2):
                    leaf = phase * LEAF_DEV + 2 * pair + half
                    nodes[leaf] = turned[half * RANK : (half + 1) * RANK].astype(bf16)
                    left, right = (coef, swapped) if half == 0 else (swapped, coef)
                    high, low = two(jnp.where(lower, left, right))
                    coefs[leaf, 0:NRHS] = high
                    coefs[leaf, NRHS : 2 * NRHS] = low
            return 0

        lax.fori_loop(0, LEAF_DEV // 8, prepare, 0)

    block = lax.broadcasted_iota(jnp.int32, (1, 4 * RANK), 1) // RANK
    left_half = lax.broadcasted_iota(jnp.int32, (RANK, 2 * RANK), 1) < RANK

    def span(quad):
        if isinstance(quad, int):
            return slice(quad * 4 * RANK, (quad + 1) * 4 * RANK)
        return pl.ds(pl.multiple_of(quad * 4 * RANK, 4 * RANK), 4 * RANK)

    def sources(quad, chunk):
        return [[far_ref[chunk * 4 + f, quad * 4 + k] for f in range(4)] for k in range(4)]

    def weights(quad):
        features = target_features(node_target_ref[:, span(quad)])
        return jnp.concatenate([jnp.where(block == k, features, 0.0) for k in range(4)], axis=0).astype(bf16)

    def values(quad, chunk, slot, targets):
        leaves = sources(quad, chunk)
        parts = []
        for f in range(4):
            one = jnp.where(left_half, nodes[leaves[0][f]], nodes[leaves[1][f]])
            other = jnp.where(left_half, nodes[leaves[2][f]], nodes[leaves[3][f]])
            parts.append(jnp.concatenate([one, other], axis=1))
        squares = product(jnp.concatenate(parts, axis=0), targets, NN)
        for row in range(0, LEAF, 64):
            high, low = two(lax.rsqrt(squares[row : row + 64]))
            highs[slot, row : row + 64] = high
            lows[slot, row : row + 64] = low

    def apply(quad, chunk, slot):
        leaves = sources(quad, chunk)
        sides = []
        for k in range(4):
            one = jnp.where(left_half, coefs[leaves[k][0]], coefs[leaves[k][1]])
            other = jnp.where(left_half, coefs[leaves[k][2]], coefs[leaves[k][3]])
            sides.append(jnp.concatenate([one, other], axis=1))
        upper = product(jnp.concatenate(sides, axis=0), highs[slot], NN)
        lower = product(jnp.concatenate([side[0:NRHS] for side in sides], axis=0), lows[slot], NN)
        field = jnp.zeros((NRHS, 4 * RANK), f32)
        for k in range(4):
            own = upper[2 * k * NRHS : (2 * k + 1) * NRHS] + upper[(2 * k + 1) * NRHS : (2 * k + 2) * NRHS]
            field = jnp.where(block == k, own + lower[k * NRHS : (k + 1) * NRHS], field)
        return field

    chunks = FAR2 // 4
    for half in range(2):
        first = weights(half)
        for chunk in range(chunks):
            values(half, chunk, half * chunks + chunk, first)

    def fields(pair, _):
        for half in range(2):
            quad = pair * 2 + half
            later = jnp.minimum(quad + 2, LEAF_DEV // 4 - 2 + half)
            targets = weights(later)
            field = jnp.zeros((NRHS, 4 * RANK), f32)
            for chunk in range(chunks):
                field = field + apply(quad, chunk, half * chunks + chunk)
                values(later, chunk, half * chunks + chunk, targets)
            field_ref[:, span(quad)] = field * inv_four_pi
        return 0

    lax.fori_loop(0, LEAF_DEV // 8, fields, 0)


def near_kernel(phase, list_ref, *refs):
    if phase == 0:
        (pack_ref, target_ref, out_ref, source, target, sides, highs, lows) = refs
        packs = (pack_ref,)
        out_ref[...] = jnp.zeros_like(out_ref)
    else:
        (far_ref, *packs, target_ref, node_target_ref, before_ref, out_ref, field_ref) = refs[:9]
        (source, target, sides, highs, lows, *far_parts) = refs[9:]
        out_ref[...] = before_ref[...]
        far_field(far_ref, packs, node_target_ref, field_ref, highs, lows, *far_parts)
        packs = packs[1:]

    def prepare(group, _):
        for leaf in [group * STEP + k for k in range(STEP)]:
            lanes = pl.ds(pl.multiple_of(leaf * LEAF, LEAF), LEAF)
            packed = pl.ds(pl.multiple_of(group * PACK + (leaf - group * STEP) * LEAF, LEAF), LEAF)
            target[leaf] = target_features(target_ref[:, lanes]).astype(bf16)
            for number, pack_ref in enumerate(packs):
                features = source_features(pack_ref[NRHS : NRHS + 8, packed])
                source[number * LEAF_DEV + leaf] = features.T.astype(bf16)
                high, low = two(pack_ref[0:NRHS, packed])
                sides[number * LEAF_DEV + leaf, 0:NRHS] = high
                sides[number * LEAF_DEV + leaf, NRHS : 2 * NRHS] = low
        return 0

    lax.fori_loop(0, LEAF_DEV // STEP, prepare, 0)

    def item(index):
        code = list_ref[0, index if phase == 0 else LIST - 1 - index]
        return lax.shift_right_logical(code, 6) & 63, code & (63 if phase == 1 else LEAF_DEV - 1)

    def values(index, slot):
        to, of = item(index)
        squares = product(source[of], target[to], NN)
        for row in range(0, LEAF, 64):
            high, low = two(lax.rsqrt(squares[row : row + 64]))
            highs[slot, row : row + 64] = high
            lows[slot, row : row + 64] = low

    def apply(index, slot):
        to, of = item(index)
        upper = product(sides[of], highs[slot], NN)
        lower = product(sides[of, 0:NRHS], lows[slot], NN)
        return to, upper[0:NRHS] + upper[NRHS : 2 * NRHS] + lower

    for slot in range(UNROLL):
        values(slot, slot)

    def step(number, _):
        results = []
        for slot in range(UNROLL):
            index = number * UNROLL + slot
            results.append(apply(index, slot))
            values(index + UNROLL, slot)
        for to, result in results:
            out_ref[to] += result
        return 0

    length = list_ref[1, phase]
    lax.fori_loop(0, lax.div(length + (UNROLL - 1), UNROLL), step, 0)


def near(phase, smem, operands):
    rows, sources = LEAF_DEV + 1, LEAF_DEV * (1 + phase)
    shapes = [jax.ShapeDtypeStruct((rows, NRHS, LEAF), f32)]
    parts = []
    if phase == 1:
        shapes.append(jax.ShapeDtypeStruct((NRHS, LEAF_DEV * RANK), f32))
        parts = [pltpu.VMEM((3 * LEAF_DEV, RANK, 2 * RANK), bf16)] * 2
    return pl.pallas_call(
        functools.partial(near_kernel, phase),
        grid=(1,),
        in_specs=[SMEM] * len(smem) + [whole(operand) for operand in operands],
        out_specs=[whole(shape) for shape in shapes],
        out_shape=shapes,
        scratch_shapes=[
            pltpu.VMEM((sources, LEAF, FEAT), bf16),
            pltpu.VMEM((rows, FEAT, LEAF), bf16),
            pltpu.VMEM((sources, 2 * NRHS, LEAF), bf16),
            pltpu.VMEM((UNROLL, LEAF, LEAF), bf16),
            pltpu.VMEM((UNROLL, LEAF, LEAF), bf16),
            *parts,
        ],
        compiler_params=LIMIT,
        cost_estimate=pl.CostEstimate(flops=20_000_000_000, bytes_accessed=4_000_000, transcendentals=14_000_000),
        name="near" + str(phase),
    )(*smem, *operands)


def couple(groups, targets):
    kernels = []
    for _, rows in groups:
        kernels.append(product(targets, source_features(rows).astype(bf16), NN))
    total = jnp.zeros((2 * NRHS, RANK), f32)
    extra = jnp.zeros((NRHS, RANK), f32)
    for (coefs, _), squares in zip(groups, kernels):
        high, low = two(lax.rsqrt(squares))
        side, rest = two(coefs)
        total = total + product(jnp.concatenate([side, rest], axis=0), high, NT)
        extra = extra + product(side, low, NT)
    return total[0:NRHS] + total[NRHS : 2 * NRHS] + extra


def down_kernel(
    mid_row_ref,
    top_mask_ref,
    top_nodes_ref,
    mid_nodes_ref,
    mid_transfer_ref,
    level_hbm,
    transfer_hbm,
    field_hbm,
    near_hbm,
    basis_hbm,
    out_hbm,
    level_ref,
    transfer_ref,
    field_ref,
    near_ref,
    basis_ref,
    out_ref,
    rows,
    tops,
    level_sem,
    side_sem,
    leaf_sem,
    out_sem,
):
    parent = lax.axis_index("clus") // GROUP
    block = 4 * GROUP
    blocks = level_ref.shape[0] // block
    leaves = 2 * GROUPS
    parts = LEAF_DEV // leaves
    copy = pltpu.make_async_copy
    level_copies = [
        copy(level_hbm.at[k * block : (k + 1) * block], level_ref.at[k * block : (k + 1) * block], level_sem.at[k])
        for k in range(blocks)
    ]
    side_copies = [copy(transfer_hbm, transfer_ref, side_sem.at[0]), copy(field_hbm, field_ref, side_sem.at[1])]
    near_copies, basis_copies, out_copies = [], [], []
    for k in range(parts):
        own = slice(k * leaves, (k + 1) * leaves)
        lanes = slice(k * leaves * LEAF, (k + 1) * leaves * LEAF)
        near_copies.append(copy(near_hbm.at[own], near_ref.at[own], leaf_sem.at[0, k]))
        basis_copies.append(copy(basis_hbm.at[own], basis_ref.at[own], leaf_sem.at[1, k]))
        out_copies.append(copy(out_ref.at[:, lanes], out_hbm.at[:, lanes], out_sem.at[k]))
    for started in level_copies + side_copies + basis_copies + near_copies:
        started.start()

    lower = lax.broadcasted_iota(jnp.int32, (1, 2 * RANK), 1) < RANK

    def features(nodes):
        target_rows(rows, nodes)
        return target_features(rows[...]).T.astype(bf16)

    def beside(left, right):
        return jnp.where(lower, left, pltpu.roll(right, RANK, 1))

    source_rows(tops, top_nodes_ref[...])
    own = jnp.zeros((3, RANK), f32)
    for top in range(top_nodes_ref.shape[1] // RANK):
        own = jnp.where(parent == top, top_nodes_ref[:, top * RANK : (top + 1) * RANK], own)
    top_targets = features(own)
    mid_targets = features(mid_nodes_ref[...])
    top_field = jnp.zeros((NRHS, RANK), f32)
    field = jnp.zeros((NRHS, RANK), f32)
    for number in range(blocks):
        level_copies[number].wait()
        groups, coefs = [], []
        for group in range(GROUP):
            first = number * block + group * 4
            picked = [level_ref[first + k] for k in range(4)]
            masked = [picked[k] * mid_row_ref[0, first + k].astype(f32) for k in range(4)]
            side = [beside(masked[0][0:NRHS], masked[1][0:NRHS]), beside(masked[2][0:NRHS], masked[3][0:NRHS])]
            node = [picked[k][NRHS : NRHS + 8] for k in range(4)]
            node = [beside(node[0], node[1]), beside(node[2], node[3])]
            groups.append((jnp.concatenate(side, axis=1), jnp.concatenate(node, axis=1)))
        for top in range(number * 4, number * 4 + 4):
            coef = level_ref[top * GROUP, 0:NRHS]
            for member in range(1, GROUP):
                coef = coef + level_ref[top * GROUP + member, 0:NRHS]
            coefs.append(coef * top_mask_ref[parent, top].astype(f32))
        swapped = [pltpu.roll(coef, RANK, 1) for coef in coefs]
        side = jnp.concatenate([jnp.where(lower, swapped[k], coefs[k + 1]) for k in (0, 2)], axis=1)
        top_field = top_field + couple([(side, tops[:, number * 4 * RANK : (number + 1) * 4 * RANK])], top_targets)
        field = field + couple(groups, mid_targets)
    field = field * inv_four_pi + fine(top_field * inv_four_pi, mid_transfer_ref[...], NN)
    for awaited in side_copies:
        awaited.wait()
    field_ref[...] += fine(field, transfer_ref[...], NN)
    for k in range(parts):
        basis_copies[k].wait()
        near_copies[k].wait()
        for leaf in range(k * leaves, (k + 1) * leaves):
            far = fine(field_ref[:, leaf * RANK : (leaf + 1) * RANK], basis_ref[leaf], NN)
            out_ref[:, leaf * LEAF : (leaf + 1) * LEAF] = far + near_ref[leaf]
        out_copies[k].start()
    for awaited in out_copies:
        awaited.wait()


def downward(mid_row, top_mask, everyone, top_nodes, mid_nodes, mid_transfer, transfer, field, near_out, basis):
    fixed = (top_nodes, mid_nodes, mid_transfer)
    blocks, parts = everyone.shape[0] // (4 * GROUP), LEAF_DEV // (2 * GROUPS)
    return pl.pallas_call(
        down_kernel,
        grid=(1,),
        in_specs=[SMEM, SMEM] + [whole(operand) for operand in fixed] + [pl.BlockSpec(memory_space=pl.ANY)] * 5,
        out_specs=pl.BlockSpec(memory_space=pl.ANY),
        out_shape=jax.ShapeDtypeStruct((NRHS, LEAF_DEV * LEAF), f32),
        scratch_shapes=[
            pltpu.VMEM(everyone.shape, f32),
            pltpu.VMEM(transfer.shape, f32),
            pltpu.VMEM(field.shape, f32),
            pltpu.VMEM(near_out.shape, f32),
            pltpu.VMEM(basis.shape, f32),
            pltpu.VMEM((NRHS, LEAF_DEV * LEAF), f32),
            pltpu.VMEM((8, RANK), f32),
            pltpu.VMEM((8, top_nodes.shape[1]), f32),
            pltpu.SemaphoreType.DMA((blocks,)),
            pltpu.SemaphoreType.DMA((2,)),
            pltpu.SemaphoreType.DMA((2, parts)),
            pltpu.SemaphoreType.DMA((parts,)),
        ],
        compiler_params=LIMIT,
        name="downward",
    )(mid_row, top_mask, *fixed, everyone, transfer, field, near_out, basis)


def shards(
    charges,
    positions,
    quad_weights,
    leaf_basis,
    leaf_nodes,
    leaf_transfer,
    mid_nodes,
    mid_transfer,
    top_nodes,
    near_list,
    near_count,
    far_list,
    mid_mask,
    top_mask,
):
    devices = lax.axis_size("clus")
    partner = [(i, i ^ 1) for i in range(devices)]
    cross = [(i, (i + 1 if i % 2 else i - 1) % devices) for i in range(devices)]
    pack, targets, node_targets, level = upward(
        charges, positions, quad_weights.reshape(1, -1), leaf_basis, leaf_nodes, leaf_transfer, mid_nodes, mid_transfer
    )
    everyone = lax.all_gather(level, "clus", axis=0, tiled=False)
    pack_partner = lax.ppermute(pack, "clus", partner)
    pack_cross = lax.ppermute(pack, "clus", cross)

    items, far_codes = lists(devices, near_list, near_count, far_list.T)
    (near_out,) = near(0, (items,), (pack, targets))
    near_out, field = near(1, (items, far_codes), (pack, pack_partner, pack_cross, targets, node_targets, near_out))
    return downward(
        mid_mask, top_mask, everyone, top_nodes, mid_nodes, mid_transfer, leaf_transfer, field, near_out, leaf_basis
    )


def solution(mesh):
    in_specs = (
        P(None, "clus"),
        P(None, "clus"),
        P("clus"),
        P("clus", None, None),
        P(None, "clus"),
        P(None, "clus"),
        P(None, "clus"),
        P(None, "clus"),
        P(),
        P("clus", None),
        P("clus"),
        P("clus", None),
        P("clus", None),
        P(),
    )
    out_specs = P(None, "clus")
    return jax.shard_map(shards, mesh=mesh, in_specs=in_specs, out_specs=out_specs, check_vma=False)
```

profile of v0, /device:TPU:24, one launch (start us, length us, event | category | flops | bytes accessed | tf_op | source)
XLA Modules:
  0.0 97.2 jit_solution(8081395521790598546)
XLA Ops:
  6.5 0.0 all-gather.3.cloned.1.call-start
  6.5 5.4 %upward.1 = (f32[40,10240]{1,0:T(8,128)}, f32[8,8192]{1,0:T(8,128)}, f32[8,2048]{1,0:T(8,128)}, f32[40,128]{1,0:T(8,128)}) custom-call(f32[32,8192]{1,0:T(8,128)} %charges_ref.1, f32[3,8192]{1,0:T(4,128)} %points_ref.1, f32[1,8192]{1,0:T(1,128)} %bitcast.5, f32[32,64,256]{2,1,0:T(8,128)} %basis_hbm.1, f32[3,2048]{1,0:T(4,128)} %nodes_ref.1, ...), custom_call_target="tpu_custom_call" | custom-call | tf_op jit(solution)/shard_map/upward/pallas_call | solution.py:148
  12.0 0.0 all-gather.3.cloned.1.call-update
  12.0 0.1 collective-permute-start
  12.1 6.5 %collective-permute-start.1 = (f32[40,10240]{1,0:T(8,128)}, f32[40,10240]{1,0:T(8,128)}, u32[]{:S(2)}, u32[]{:S(2)}) collective-permute-start(f32[40,10240]{1,0:T(8,128)} %get-tuple-element.16.refs_0_.refs_1_), channel_id=1, source_target_pairs={{0,127},{1,2},{2,1},{3,4},{4,3},{5,6},{6,5},{7,8},{8,7},{9,10},{10... | collective-permute-start | bytes 4915208 | tf_op jit(solution)/shard_map/ppermute | solution.py:576
  18.6 2.1 %lists.1 = (s32[2,1024]{1,0:T(2,128)}, s32[16,32]{1,0:T(8,128)}) custom-call(s32[32,27]{1,0:T(8,128)} %near_ref.1, s32[1,32]{1,0:T(1,128)} %bitcast.7, s32[16,32]{1,0:T(8,128)} %bitcast.6), custom_call_target="tpu_custom_call" | custom-call | tf_op jit(solution)/shard_map/lists/pallas_call | solution.py:223
  20.7 19.7 %near0.1.refs_6_ = f32[33,32,256]{2,1,0:T(8,128)} custom-call(s32[2,1024]{1,0:T(2,128)} %get-tuple-element.14.list_ref, f32[40,10240]{1,0:T(8,128)} %get-tuple-element.16.refs_0_.refs_1_, f32[8,8192]{1,0:T(8,128)} %get-tuple-element.17.refs_1_.refs_4_), custom_call_target="tpu_custom_call" | custom-call | flops 20000000000 | bytes 4000000 | tf_op jit(solution)/shard_map/near0/pallas_call | solution.py:392
  40.3 0.0 collective-permute-done.refs_2_
  40.4 0.0 collective-permute-done.1.refs_3_
  40.4 42.5 %near1.1 = (f32[33,32,256]{2,1,0:T(8,128)}, f32[32,2048]{1,0:T(8,128)}) custom-call(s32[2,1024]{1,0:T(2,128)} %get-tuple-element.14.list_ref, s32[16,32]{1,0:T(8,128)} %get-tuple-element.15.refs_0_, f32[40,10240]{1,0:T(8,128)} %get-tuple-element.16.refs_0_.refs_1_, f32[40,10240]{1,0:T(8,128)} %collective-permute-done.refs_2_, ...), custom_call_target="tpu_custom_call" | custom-call | flops 20000000000 | bytes 4000000 | tf_op jit(solution)/shard_map/near1/pallas_call | solution.py:392
  82.8 0.0 all-gather.3.cloned.1.call-done
  82.8 7.5 %downward.1 = f32[32,8192]{1,0:T(8,128)} custom-call(s32[1,128]{1,0:T(1,128)} %mid_row_ref.1, s32[16,16]{1,0:T(8,128)} %top_mask_ref.1, f32[3,1024]{1,0:T(4,128)} %top_nodes_ref.1, f32[3,64]{1,0:T(4,128)} %mid_nodes_ref.3, f32[64,64]{1,0:T(8,128)} %mid_transfer_ref.3, f32[128,40,128]{2,1,0:T(8,128)} %bitcast.4, f32[64,2048]{1,0:T(8,128)} %transfer_hbm.1, ...), custom_call_target="tpu_custom_call" | custom-call | tf_op jit(solution)/shard_map/downward/pallas_call | solution.py:527
Async XLA Ops:
  6.5 76.3 %all-gather.3.cloned.1.call-start = ((), (), s32[]{:S(2)}) async-start(), calls=%async_computation | async-start | bytes 2641920 | tf_op jit(solution)/shard_map/all_gather | solution.py:574
  12.0 28.4 %collective-permute-start = (f32[40,10240]{1,0:T(8,128)}, f32[40,10240]{1,0:T(8,128)}, u32[]{:S(2)}, u32[]{:S(2)}) collective-permute-start(f32[40,10240]{1,0:T(8,128)} %get-tuple-element.16.refs_0_.refs_1_), channel_id=1, source_target_pairs={{0,1},{1,0},{2,3},{3,2},{4,5},{5,4},{6,7},{7,6},{8,9},{9,8},{10,11... | collective-permute-start | bytes 4915208 | tf_op jit(solution)/shard_map/ppermute | solution.py:575
  12.1 28.3 %collective-permute-start.1 = (f32[40,10240]{1,0:T(8,128)}, f32[40,10240]{1,0:T(8,128)}, u32[]{:S(2)}, u32[]{:S(2)}) collective-permute-start(f32[40,10240]{1,0:T(8,128)} %get-tuple-element.16.refs_0_.refs_1_), channel_id=1, source_target_pairs={{0,127},{1,2},{2,1},{3,4},{4,3},{5,6},{6,5},{7,8},{8,7},{9,10},{10... | collective-permute-start | bytes 4915208 | tf_op jit(solution)/shard_map/ppermute | solution.py:576
Sparse Core Ops, SparseCore 0:
  12.1 65.9 all-gather.2
where the time goes:
time: 98.1 us; the launch traced here: 97.2 us
  Pallas kernels  77.1 us (79%)
  between operations  13.4 us (14%)
  starting transfers between devices  6.6 us (7%)
    pallas_call x2, Pallas kernels, near(): pl.pallas_call(functools.partial(near_kernel, phase), grid=(1,), in_specs...  62.2 us
    pallas_call x1, Pallas kernels, downward(): pl.pallas_call(down_kernel, grid=(1,), in_specs=[SMEM, SMEM] + [whole(ope...  7.47 us
    ppermute x1, starting transfers between devices, shards(): pack_cross = lax.ppermute(pack, 'clus', cross)  6.51 us
    pallas_call x1, Pallas kernels, upward(): pl.pallas_call(upward_kernel, grid=(steps,), in_specs=[lanes(NRHS, wide),...  5.43 us
    pallas_call x1, Pallas kernels, lists(): pl.pallas_call(functools.partial(lists_kernel, devices), grid=(1,), in_sp...  2.07 us
  transfers between devices with their start and end apart: 3, of which 0 were waited for; matrix products, arithmetic and copies ran while one was open for 0% of the time, Pallas kernels for 66%

commit v1 on v0

--- a/solution.py
+++ b/solution.py
@@ -572,10 +572,11 @@
         charges, positions, quad_weights.reshape(1, -1), leaf_basis, leaf_nodes, leaf_transfer, mid_nodes, mid_transfer
     )
     everyone = lax.all_gather(level, "clus", axis=0, tiled=False)
+    items, far_codes = lists(devices, near_list, near_count, far_list.T)
+    pack, items = lax.optimization_barrier((pack, items))
     pack_partner = lax.ppermute(pack, "clus", partner)
     pack_cross = lax.ppermute(pack, "clus", cross)
 
-    items, far_codes = lists(devices, near_list, near_count, far_list.T)
     (near_out,) = near(0, (items,), (pack, targets))
     near_out, field = near(1, (items, far_codes), (pack, pack_partner, pack_cross, targets, node_targets, near_out))
     return downward(

time: 98.1 us -> 99.9 us (1.018)
  the two profiles are of different devices: /device:TPU:24 before, /device:TPU:1 now
where the time goes in v1:
time: 99.9 us; the launch traced here: 98.9 us
  Pallas kernels  82.9 us (83%)
  between operations  13.4 us (13%)
  starting transfers between devices  2.61 us (3%)
    pallas_call x2, Pallas kernels, near(): pl.pallas_call(functools.partial(near_kernel, phase), grid=(1,), in_specs...  67.9 us
    pallas_call x1, Pallas kernels, downward(): pl.pallas_call(down_kernel, grid=(1,), in_specs=[SMEM, SMEM] + [whole(ope...  7.47 us
    pallas_call x1, Pallas kernels, upward(): pl.pallas_call(upward_kernel, grid=(steps,), in_specs=[lanes(NRHS, wide),...  5.44 us
    pallas_call x1, Pallas kernels, lists(): pl.pallas_call(functools.partial(lists_kernel, devices), grid=(1,), in_sp...  2.07 us
  transfers between devices with their start and end apart: 3, of which 0 were waited for; matrix products, arithmetic and copies ran while one was open for 0% of the time, Pallas kernels for 71%

profile of v1, /device:TPU:1, one launch (start us, length us, event | category | flops | bytes accessed | tf_op | source)
XLA Modules:
  0.0 98.9 jit_solution(5254432322147283133)
XLA Ops:
  6.5 0.0 all-gather.3.cloned.1.call-start
  6.5 5.4 %upward.1 = (f32[40,10240]{1,0:T(8,128)}, f32[8,8192]{1,0:T(8,128)}, f32[8,2048]{1,0:T(8,128)}, f32[40,128]{1,0:T(8,128)}) custom-call(f32[32,8192]{1,0:T(8,128)} %charges_ref.1, f32[3,8192]{1,0:T(4,128)} %points_ref.1, f32[1,8192]{1,0:T(1,128)} %bitcast.5, f32[32,64,256]{2,1,0:T(8,128)} %basis_hbm.1, f32[3,2048]{1,0:T(4,128)} %nodes_ref.1, ...), custom_call_target="tpu_custom_call" | custom-call | tf_op jit(solution)/shard_map/upward/pallas_call | solution.py:148
  12.0 0.0 all-gather.3.cloned.1.call-update
  12.0 2.1 %lists.1 = (s32[2,1024]{1,0:T(2,128)}, s32[16,32]{1,0:T(8,128)}) custom-call(s32[32,27]{1,0:T(8,128)} %near_ref.1, s32[1,32]{1,0:T(1,128)} %bitcast.7, s32[16,32]{1,0:T(8,128)} %bitcast.6), custom_call_target="tpu_custom_call" | custom-call | tf_op jit(solution)/shard_map/lists/pallas_call | solution.py:223
  14.1 1.4 %collective-permute-start = (f32[40,10240]{1,0:T(8,128)}, f32[40,10240]{1,0:T(8,128)}, u32[]{:S(2)}, u32[]{:S(2)}) collective-permute-start(f32[40,10240]{1,0:T(8,128)} %get-tuple-element.20.refs_0_.refs_1_), channel_id=1, source_target_pairs={{0,1},{1,0},{2,3},{3,2},{4,5},{5,4},{6,7},{7,6},{8,9},{9,8},{10,11... | collective-permute-start | bytes 4915208 | tf_op jit(solution)/shard_map/ppermute | solution.py:577
  15.5 1.2 %collective-permute-start.1 = (f32[40,10240]{1,0:T(8,128)}, f32[40,10240]{1,0:T(8,128)}, u32[]{:S(2)}, u32[]{:S(2)}) collective-permute-start(f32[40,10240]{1,0:T(8,128)} %get-tuple-element.20.refs_0_.refs_1_), channel_id=1, source_target_pairs={{0,127},{1,2},{2,1},{3,4},{4,3},{5,6},{6,5},{7,8},{8,7},{9,10},{10... | collective-permute-start | bytes 4915208 | tf_op jit(solution)/shard_map/ppermute | solution.py:578
  16.7 23.1 %near0.1.refs_6_ = f32[33,32,256]{2,1,0:T(8,128)} custom-call(s32[2,1024]{1,0:T(2,128)} %get-tuple-element.18.list_ref, f32[40,10240]{1,0:T(8,128)} %get-tuple-element.20.refs_0_.refs_1_, f32[8,8192]{1,0:T(8,128)} %get-tuple-element.21.refs_1_.refs_4_), custom_call_target="tpu_custom_call" | custom-call | flops 20000000000 | bytes 4000000 | tf_op jit(solution)/shard_map/near0/pallas_call | solution.py:392
  39.8 0.0 collective-permute-done.refs_2_
  39.8 0.0 collective-permute-done.1.refs_3_
  39.8 44.8 %near1.1 = (f32[33,32,256]{2,1,0:T(8,128)}, f32[32,2048]{1,0:T(8,128)}) custom-call(s32[2,1024]{1,0:T(2,128)} %get-tuple-element.18.list_ref, s32[16,32]{1,0:T(8,128)} %get-tuple-element.19.refs_0_, f32[40,10240]{1,0:T(8,128)} %get-tuple-element.20.refs_0_.refs_1_, f32[40,10240]{1,0:T(8,128)} %collective-permute-done.refs_2_, ...), custom_call_target="tpu_custom_call" | custom-call | flops 20000000000 | bytes 4000000 | tf_op jit(solution)/shard_map/near1/pallas_call | solution.py:392
  84.6 0.0 all-gather.3.cloned.1.call-done
  84.6 7.5 %downward.1 = f32[32,8192]{1,0:T(8,128)} custom-call(s32[1,128]{1,0:T(1,128)} %mid_row_ref.1, s32[16,16]{1,0:T(8,128)} %top_mask_ref.1, f32[3,1024]{1,0:T(4,128)} %top_nodes_ref.1, f32[3,64]{1,0:T(4,128)} %mid_nodes_ref.3, f32[64,64]{1,0:T(8,128)} %mid_transfer_ref.3, f32[128,40,128]{2,1,0:T(8,128)} %bitcast.4, f32[64,2048]{1,0:T(8,128)} %transfer_hbm.1, ...), custom_call_target="tpu_custom_call" | custom-call | tf_op jit(solution)/shard_map/downward/pallas_call | solution.py:527
Async XLA Ops:
  6.5 78.1 %all-gather.3.cloned.1.call-start = ((), (), s32[]{:S(2)}) async-start(), calls=%async_computation | async-start | bytes 2641920 | tf_op jit(solution)/shard_map/all_gather | solution.py:574
  14.1 25.7 %collective-permute-start = (f32[40,10240]{1,0:T(8,128)}, f32[40,10240]{1,0:T(8,128)}, u32[]{:S(2)}, u32[]{:S(2)}) collective-permute-start(f32[40,10240]{1,0:T(8,128)} %get-tuple-element.20.refs_0_.refs_1_), channel_id=1, source_target_pairs={{0,1},{1,0},{2,3},{3,2},{4,5},{5,4},{6,7},{7,6},{8,9},{9,8},{10,11... | collective-permute-start | bytes 4915208 | tf_op jit(solution)/shard_map/ppermute | solution.py:577
  15.5 24.3 %collective-permute-start.1 = (f32[40,10240]{1,0:T(8,128)}, f32[40,10240]{1,0:T(8,128)}, u32[]{:S(2)}, u32[]{:S(2)}) collective-permute-start(f32[40,10240]{1,0:T(8,128)} %get-tuple-element.20.refs_0_.refs_1_), channel_id=1, source_target_pairs={{0,127},{1,2},{2,1},{3,4},{4,3},{5,6},{6,5},{7,8},{8,7},{9,10},{10... | collective-permute-start | bytes 4915208 | tf_op jit(solution)/shard_map/ppermute | solution.py:578
Sparse Core Ops, SparseCore 0:
  12.1 69.3 all-gather.2
